TPU v7x, 512 devices: a whole 4x4x16 slice. The times are simulated.
512 devices in a mesh: pipe: 4 (over y), seq: 16 (over z), tensor: 8 (over x, core).
Axes of the slice: x: 4, y: 4, z: 16, core: 2. Of those that a mesh axis runs over, the one named last changes fastest.
Arguments:
- layer_input: bfloat16 [4, 2048, 8192], P('pipe', 'seq', 'tensor'), may hold values from -320 to 320
- conv_out: bfloat16 [4, 2048, 8192], P('pipe', 'seq', 'tensor'), may hold values from -8 to 8
- act_grad: bfloat16 [4, 2048, 8192], P('pipe', 'seq', 'tensor'), may hold values from -6 to 6
- conv_kernel: bfloat16 [4, 4, 8192], P('pipe', None, 'tensor'), may hold values from -3 to 3
- in_proj: bfloat16 [4, 8192, 8192], P('pipe', 'seq', 'tensor'), may hold values from -0.0625 to 0.0625
- sketch_matrix: bfloat16 [4, 8192, 512], P('pipe', 'tensor'), may hold values from -0.0625 to 0.0625
Outputs:
- passed_grad: bfloat16 [4, 2048, 8192], P('pipe', 'tensor', 'seq')
- basis: bfloat16 [4, 8192, 512], P('pipe', 'tensor')
All inputs are finite; a program needn't handle non-finite values.
Results may differ from a plain program's by a relative error of at most 0.017.
Values may be sent and summed in bfloat16 or wider, within the bound.
No kernel may reach another device: no remote copies, remote signals or barrier semaphores. Data moves between devices by JAX's collectives and lax.ppermute only.
A program may use at most 64 MiB of HBM per device.

v0:
```python
import math
import jax
import jax.numpy as jnp
from jax import lax
from jax.sharding import PartitionSpec as P

D = 8192


def passed_along(block, axis, distance):
    devices = range(lax.axis_size(axis))
    route = [(i - distance, i) for i in devices if i - distance in devices]
    return lax.ppermute(block, axis, route)


def shifted(value, axis, by):
    count = lax.axis_size(axis)
    return lax.ppermute(value, axis, [(i, (i + by) % count) for i in range(count)])


def finish_basis(sketch, gram):
    low = jnp.linalg.cholesky(gram)
    ortho_t = lax.linalg.triangular_solve(low, sketch.T, left_side=True, lower=True)
    return (ortho_t.T * math.sqrt(D)).astype(jnp.bfloat16)


def local(layer_input, conv_out, act_grad, conv_kernel, in_proj, sketch_matrix):
    acts = layer_input[0]
    kernel = conv_kernel[0]
    weights = in_proj[0]
    test_matrix = sketch_matrix[0]
    tok_rows = acts.shape[0]
    taps = kernel.shape[0]
    pval = conv_out[0].astype(jnp.float32)
    sig = jax.nn.sigmoid(pval)
    pre_grad = act_grad[0].astype(jnp.float32) * sig * (1.0 + pval * (1.0 - sig))
    ahead = passed_along(pre_grad[: taps - 1], "seq", -1)
    extended = jnp.concatenate([pre_grad, ahead], axis=0)
    total = jnp.zeros(pre_grad.shape, jnp.float32)
    for tap in range(taps):
        total = total + kernel[tap].astype(jnp.float32) * extended[tap : tap + tok_rows]
    in_grad = total.astype(jnp.bfloat16)
    partial_grad = lax.dot_general(
        lax.all_gather(in_grad, "seq", axis=0, tiled=True),
        weights,
        (((1,), (1,)), ((), ())),
        preferred_element_type=jnp.float32,
    )
    input_grad = lax.psum_scatter(
        partial_grad.astype(jnp.bfloat16), "tensor", scatter_dimension=0, tiled=True
    )
    passed = shifted(input_grad, "pipe", -1)
    row_terms = jnp.dot(in_grad, test_matrix, preferred_element_type=jnp.float32)
    sketch_rows = lax.psum(row_terms, "tensor").astype(jnp.bfloat16)
    sketch_part = lax.dot_general(
        acts, sketch_rows, (((0,), (0,)), ((), ())), preferred_element_type=jnp.float32
    )
    sketch = lax.psum(sketch_part, "seq")
    gram_part = jnp.dot(sketch.T, sketch, precision=lax.Precision.HIGHEST)
    gram = lax.psum(gram_part, "tensor")
    basis = finish_basis(sketch, gram)
    return (passed[None], basis[None])


def solution(mesh):
    placed = (
        P("pipe", "seq", "tensor"),
        P("pipe", "seq", "tensor"),
        P("pipe", "seq", "tensor"),
        P("pipe", None, "tensor"),
        P("pipe", "seq", "tensor"),
        P("pipe", "tensor", None),
    )
    return jax.shard_map(
        local,
        mesh=mesh,
        in_specs=placed,
        out_specs=(P("pipe", "tensor", "seq"), P("pipe", "tensor", None)),
        check_vma=False,
    )
```

profile of v0, /device:TPU:26, one launch (start us, length us, event | category | flops | bytes accessed | tf_op | source)
XLA Modules:
  0.0 470.1 jit_solution(17740369245081746752)
XLA Ops:
  7.2 1.4 fusion.30
  8.7 1.3 collective-permute-start
  10.0 0.9 slice_convert_fusion.3
  10.8 3.5 collective-permute-done
  14.9 24.3 %all-reduce.8 = bf16[128,512]{1,0:T(8,128)(2,1)S(1)} all-reduce(f32[128,512]{1,0:T(8,128)S(1)} %fusion.15), channel_id=1, replica_groups=mesh['pipe'=4,'seq'=16,'tensor'=8] {'tensor'}, use_global_device_ids=true, to_apply=%region_1.0 | all-reduce | flops 65536 | bytes 393216 | tf_op jit(solution)/shard_map/psum | solution.py:54
  39.2 1.8 convolution_bitcast_fusion
  41.0 149.0 %all-reduce.5.cloned.1.call-done = f32[1024,512]{0,1:T(8,128)} async-done(((f32[1024,512]{0,1:T(8,128)}), f32[1024,512]{0,1:T(8,128)}) %all-reduce.5.cloned.1.call-update) | async-done | bytes 2097168 | tf_op jit(solution)/shard_map/psum | solution.py:58
  190.0 6.7 %fusion.56 = f32[512,512]{0,1:T(8,128)} fusion(f32[1024,512]{0,1:T(8,128)} %all-reduce.5.cloned.1.call-done), kind=kOutput, calls=%fused_computation.103 | convolution fusion | flops 3221225472 | bytes 3145728 | tf_op jit(solution)/shard_map/dot_general | solution.py:59
  196.8 0.7 all-gather.2.cloned.1.call-update
  198.0 70.5 %all-reduce.7.cloned.1.call-done = f32[512,512]{0,1:T(8,128)} async-done(((f32[512,512]{0,1:T(8,128)}), f32[512,512]{0,1:T(8,128)}) %all-reduce.7.cloned.1.call-update) | async-done | bytes 1048592 | tf_op jit(solution)/shard_map/psum | solution.py:60
  268.5 1.6 copy.9
  270.4 1.0 copy-done.7
  271.4 11.7 %cholesky.104 = f32[128,128]{1,0:T(8,128)S(1)} custom-call(f32[128,128]{1,0:T(8,128)S(1)} %cholesky.266), custom_call_target="Cholesky" | custom-call | tf_op jit(solution)/shard_map/jit(cholesky)/cholesky | solution.py:22
  283.3 9.8 %custom-call.30 = f32[1,128,128]{1,2,0:T(8,128)S(1)} custom-call(f32[1,128,128]{2,1,0:T(8,128)S(1)} %get-tuple-element.31), custom_call_target="InvertDiagBlocksLowerTriangular" | custom-call | tf_op jit(solution)/shard_map/jit(cholesky)/cholesky | solution.py:22
  293.1 1.2 constant_dynamic-update-slice_fusion.3
  294.4 1.3 convolution_subtract_fusion.2
  295.6 11.7 %cholesky.217 = f32[128,128]{1,0:T(8,128)S(1)} custom-call(f32[128,128]{1,0:T(8,128)S(1)} %cholesky.270), custom_call_target="Cholesky" | custom-call | tf_op jit(solution)/shard_map/jit(cholesky)/cholesky | solution.py:22
  307.4 10.0 %custom-call.31 = f32[1,128,128]{1,2,0:T(8,128)S(1)} custom-call(f32[1,128,128]{2,1,0:T(8,128)S(1)} %get-tuple-element.28), custom_call_target="InvertDiagBlocksLowerTriangular" | custom-call | tf_op jit(solution)/shard_map/jit(cholesky)/cholesky | solution.py:22
  317.6 1.4 convolution_subtract_fusion.3
  319.1 11.7 %cholesky.238 = f32[128,128]{1,0:T(8,128)S(1)} custom-call(f32[128,128]{1,0:T(8,128)S(1)} %cholesky.275), custom_call_target="Cholesky" | custom-call | tf_op jit(solution)/shard_map/jit(cholesky)/cholesky | solution.py:22
  330.8 21.4 %all-gather.2.cloned.1.call-done = bf16[2048,1024]{1,0:T(8,128)(2,1)} async-done(((bf16[128,1024]{1,0:T(8,128)(2,1)}), bf16[2048,1024]{1,0:T(8,128)(2,1)}) %all-gather.2.cloned.1.call-update) | async-done | bytes 4194320 | tf_op jit(solution)/shard_map/all_gather | solution.py:44
  352.2 5.9 %convolution_convert_fusion = bf16[2048,512]{1,0:T(8,128)(2,1)} fusion(bf16[2048,1024]{1,0:T(8,128)(2,1)} %all-gather.2.cloned.1.call-done, bf16[1,512,1024]{2,1,0:T(8,128)(2,1)S(1)} %copy-done), kind=kOutput, calls=%fused_computation.2 | convolution fusion | flops 2148532224 | bytes 7340032 | tf_op jit(solution)/shard_map/dot_general | solution.py:43
  358.1 0.6 select_reduce_fusion.1
  358.8 9.8 %custom-call.32 = f32[1,128,128]{1,2,0:T(8,128)S(1)} custom-call(f32[1,128,128]{2,1,0:T(8,128)S(1)} %get-tuple-element.25), custom_call_target="InvertDiagBlocksLowerTriangular" | custom-call | tf_op jit(solution)/shard_map/jit(cholesky)/cholesky | solution.py:22
  368.6 0.8 convolution_dynamic-update-slice_fusion.1
  369.4 1.5 convolution_subtract_fusion.4
  370.9 11.9 %cholesky.255 = f32[128,128]{1,0:T(8,128)S(1)} custom-call(f32[128,128]{1,0:T(8,128)S(1)} %convolution_subtract_fusion.4), custom_call_target="Cholesky" | custom-call | tf_op jit(solution)/shard_map/jit(cholesky)/cholesky | solution.py:22
  382.8 0.6 compare_reduce_fusion.2
  384.8 0.6 compare_reduce_fusion.1
  386.1 0.6 select_reduce_fusion
  386.7 0.6 compare_reduce_fusion
  388.0 2.3 select_select_fusion
  390.3 13.6 %while.1 = (s32[]{:T(128)}, f32[512,512]{1,0:T(8,128)}, s32[4,2]{0,1:T(2,128)S(1)}, f32[4,128,128]{2,1,0:T(8,128)}, s32[]{:T(128)}) while((s32[]{:T(128)}, f32[512,512]{1,0:T(8,128)}, s32[4,2]{0,1:T(2,128)S(1)}, f32[4,128,128]{2,1,0:T(8,128)}, s32[]{:T(128)}) %tuple.35), condition=%wide.while_cond, body=%wide.while_body.sunk | while | flops 2 | bytes 132205 | solution.py:23
  390.9 2.8 bitcast_dynamic-update-slice_fusion.2
  394.4 2.8 bitcast_dynamic-update-slice_fusion.2
  397.8 2.8 bitcast_dynamic-update-slice_fusion.2
  401.2 2.8 bitcast_dynamic-update-slice_fusion.2
  404.0 40.1 %custom-call.33 = f32[4,128,128]{1,2,0:T(8,128)S(1)} custom-call(f32[4,128,128]{2,1,0:T(8,128)} %get-tuple-element.9), custom_call_target="InvertDiagBlocksLowerTriangular" | custom-call | tf_op jit(solution)/shard_map/triangular_solve | solution.py:23
  444.8 1.5 convolution_subtract_fusion.1
  446.9 1.8 convolution_subtract_fusion
  449.4 0.8 copy-done.5
  450.1 2.8 fusion.7
  453.0 2.4 collective-permute-start.1
  455.4 1.7 fusion.44
  457.1 1.6 fusion.10
  458.8 1.3 copy.10
  460.1 2.6 collective-permute-done.1
  462.7 0.7 copy.32
  (53 shorter events, 6.3 us)
Async XLA Ops:
  7.2 345.0 %copy-start = (bf16[1,512,1024]{2,1,0:T(8,128)(2,1)S(1)}, bf16[1,512,1024]{2,1,0:T(8,128)(2,1)}, u32[]{:S(2)}) copy-start(bf16[1,512,1024]{2,1,0:T(8,128)(2,1)} %param.10) | copy-start | bytes 3145732
  7.2 7.4 %copy-start.9 = (bf16[1,1024,512]{2,1,0:T(8,128)(2,1)S(1)}, bf16[1,1024,512]{2,1,0:T(8,128)(2,1)}, u32[]{:S(2)}) copy-start(bf16[1,1024,512]{2,1,0:T(8,128)(2,1)} %param.11) | copy-start | bytes 3145732
  7.2 32.0 %copy-start.10 = (bf16[1,128,1024]{2,1,0:T(8,128)(2,1)S(1)}, bf16[1,128,1024]{2,1,0:T(8,128)(2,1)}, u32[]{:S(2)}) copy-start(bf16[1,128,1024]{2,1,0:T(8,128)(2,1)} %param.6) | copy-start | bytes 786436
  7.2 182.8 %all-reduce.5.cloned.1.call-start = ((), (), s32[]{:S(2)}) async-start(), calls=%async_computation.3 | async-start | bytes 4194304 | tf_op jit(solution)/shard_map/psum | solution.py:58
  8.7 5.6 %collective-permute-start = (f32[3,1024]{1,0:T(4,128)S(1)}, f32[3,1024]{1,0:T(4,128)S(1)}, u32[]{:S(2)}, u32[]{:S(2)}) collective-permute-start(f32[3,1024]{1,0:T(4,128)S(1)} %slice.150), channel_id=1, source_target_pairs={{8,0},{16,8},{24,16},{32,24},{40,32},{48,40},{56,48},{64,56},{72,6... | collective-permute-start | bytes 36872 | tf_op jit(solution)/shard_map/ppermute | solution.py:13
  14.5 26.4 %copy-start.8 = (bf16[128,1024]{1,0:T(8,128)(2,1)}, bf16[128,1024]{1,0:T(8,128)(2,1)S(1)}, u32[]{:S(2)}) copy-start(bf16[128,1024]{1,0:T(8,128)(2,1)S(1)} %fusion.22) | copy-start | bytes 786436
  41.0 227.5 %all-reduce.7.cloned.1.call-start = ((), (), s32[]{:S(2)}) async-start(), calls=%async_computation.4 | async-start | bytes 2097152 | tf_op jit(solution)/shard_map/psum | solution.py:60
  196.8 155.4 %all-gather.2.cloned.1.call-start = ((), (), s32[]{:S(2)}) async-start(), calls=%async_computation.1 | async-start | bytes 4456448 | tf_op jit(solution)/shard_map/all_gather | solution.py:44
  197.5 255.5 %reduce-scatter.2.cloned.1.call-start = ((), (), s32[]{:S(2)}) async-start(), calls=%async_computation.2 | async-start | bytes 2359296 | tf_op jit(solution)/shard_map/reduce_scatter | solution.py:49
  268.5 1.7 copy-start.6
  270.4 1.0 copy-start.7
  317.6 40.5 %copy-start.4 = (f32[512,512]{1,0:T(8,128)}, f32[512,512]{1,0:T(8,128)S(1)}, u32[]{:S(2)}) copy-start(f32[512,512]{1,0:T(8,128)S(1)} %convolution_dynamic-update-slice_fusion) | copy-start | bytes 3145732
  358.1 86.0 %copy-start.1 = (f32[1024,512]{0,1:T(8,128)S(1)}, f32[1024,512]{0,1:T(8,128)}, u32[]{:S(2)}) copy-start(f32[1024,512]{0,1:T(8,128)} %all-reduce.5.cloned.1.call-done) | copy-start | bytes 6291460
  444.8 4.6 copy-start.2
  446.9 2.4 copy-start.3
  449.3 0.8 copy-start.5
  453.0 9.7 %collective-permute-start.1 = (bf16[256,512]{1,0:T(8,128)(2,1)}, bf16[256,512]{1,0:T(8,128)(2,1)S(1)}, u32[]{:S(2)}, u32[]{:S(2)}) collective-permute-start(bf16[256,512]{1,0:T(8,128)(2,1)} %reduce-scatter.2.cloned.1.call-done), channel_id=1, source_target_pairs={{0,384},{128,0},{256,128},{384,256},{1,385},{129,1},{257,129},{385... | collective-permute-start | bytes 786440 | tf_op jit(solution)/shard_map/ppermute | solution.py:18
Sparse Core Ops, SparseCore 0:
  41.1 148.8 all-reduce.4
  196.9 71.6 all-reduce.6
  271.2 80.9 all-gather.1
  358.2 33.6 reduce-scatter.1
where the time goes:
time: 475 us; the launch traced here: 470 us
  waiting for transfers between devices  248 us (52%)
  other arithmetic  127 us (27%)
  matrix products  30.9 us (7%)
  blocking collectives  24.3 us (5%)
  local copies, waits for them, and re-layouts  19.3 us (4%)
  between operations  17 us (4%)
    psum x1, waiting for transfers between devices, local(): sketch = lax.psum(sketch_part, 'seq')  149 us
    another operation x14, other arithmetic, finish_basis(): low = jnp.linalg.cholesky(gram)  79.9 us
    psum x1, waiting for transfers between devices, local(): gram = lax.psum(gram_part, 'tensor')  70.5 us
    another operation x3, other arithmetic, finish_basis(): lax.linalg.triangular_solve(low, sketch.T, left_side=True, lower=True)  42.5 us
    psum x1, blocking collectives, local(): sketch_rows = lax.psum(row_terms, 'tensor').astype(jnp.bfloat16)  24.3 us
    all_gather x1, waiting for transfers between devices, local(): lax.all_gather(in_grad, 'seq', axis=0, tiled=True)  21.4 us
    another operation x12, local copies, waits for them, and re-layouts  13.6 us
    another operation x7, matrix products, finish_basis(): lax.linalg.triangular_solve(low, sketch.T, left_side=True, lower=True)  9.66 us
  transfers between devices with their start and end apart: 6, of which 5 were waited for; matrix products, arithmetic and copies ran while one was open for 34% of the time, Pallas kernels for 0%

commit v1 on v0

--- a/solution.py
+++ b/solution.py
@@ -57,7 +57,7 @@
     )
     sketch = lax.psum(sketch_part, "seq")
     gram_part = jnp.dot(sketch.T, sketch, precision=lax.Precision.HIGHEST)
-    gram = lax.psum(gram_part, "tensor")
+    gram = lax.all_gather(gram_part, axis_name="tensor").sum(axis=0)
     basis = finish_basis(sketch, gram)
     return (passed[None], basis[None])
 

time: 475 us -> 518 us (1.091)
  the two profiles are of different devices: /device:TPU:26 before, /device:TPU:1 now
where the time goes in v1:
time: 518 us; the launch traced here: 511 us
  waiting for transfers between devices  280 us (54%)
  other arithmetic  131 us (25%)
  blocking collectives  30.7 us (6%)
  matrix products  29.5 us (6%)
  local copies, waits for them, and re-layouts  18.6 us (4%)
  between operations  16.9 us (3%)
  starting transfers between devices  5.3 us (1%)
    psum x1, waiting for transfers between devices, local(): sketch = lax.psum(sketch_part, 'seq')  137 us
    another operation x14, other arithmetic, finish_basis(): low = jnp.linalg.cholesky(gram)  80 us
    all_gather x1, waiting for transfers between devices, local(): gram = lax.all_gather(gram_part, axis_name='tensor').sum(axis=0)  53.9 us
    another operation x3, other arithmetic, finish_basis(): lax.linalg.triangular_solve(low, sketch.T, left_side=True, lower=True)  42.5 us
    all_gather x1, waiting for transfers between devices, local(): lax.all_gather(in_grad, 'seq', axis=0, tiled=True)  42 us
    reduce_scatter x1, waiting for transfers between devices, local(): lax.psum_scatter(partial_grad.astype(jnp.bfloat16), 'tensor', scatter_dim...  40.2 us
    psum x1, blocking collectives, local(): sketch_rows = lax.psum(row_terms, 'tensor').astype(jnp.bfloat16)  30.7 us
    another operation x12, local copies, waits for them, and re-layouts  14.1 us
  transfers between devices with their start and end apart: 6, of which 6 were waited for; matrix products, arithmetic and copies ran while one was open for 3% of the time, Pallas kernels for 0%

profile of v1, /device:TPU:1, one launch (start us, length us, event | category | flops | bytes accessed | tf_op | source)
XLA Modules:
  0.0 511.5 jit_solution(854500650996299584)
XLA Ops:
  7.2 1.4 fusion.30
  8.7 1.3 collective-permute-start
  10.0 0.9 slice_convert_fusion.3
  10.8 3.3 collective-permute-done
  14.1 0.9 fusion.22
  15.2 1.3 fusion.15
  16.4 30.7 %all-reduce.5 = bf16[128,512]{1,0:T(8,128)(2,1)S(1)} all-reduce(f32[128,512]{1,0:T(8,128)S(1)} %fusion.15), channel_id=1, replica_groups=mesh['pipe'=4,'seq'=16,'tensor'=8] {'tensor'}, use_global_device_ids=true, to_apply=%region_1.0 | all-reduce | flops 65536 | bytes 393216 | tf_op jit(solution)/shard_map/psum | solution.py:54
  47.2 1.8 convolution_bitcast_fusion
  49.1 42.0 %all-gather.4.cloned.1.call-done = bf16[2048,1024]{1,0:T(8,128)(2,1)} async-done(((bf16[128,1024]{1,0:T(8,128)(2,1)}), bf16[2048,1024]{1,0:T(8,128)(2,1)}) %all-gather.4.cloned.1.call-update) | async-done | bytes 4194320 | tf_op jit(solution)/shard_map/all_gather | solution.py:44
  91.0 5.9 %convolution_convert_fusion = bf16[2048,512]{1,0:T(8,128)(2,1)} fusion(bf16[2048,1024]{1,0:T(8,128)(2,1)} %all-gather.4.cloned.1.call-done, bf16[1,512,1024]{2,1,0:T(8,128)(2,1)S(1)} %copy-done), kind=kOutput, calls=%fused_computation.2 | convolution fusion | flops 2148532224 | bytes 7340032 | tf_op jit(solution)/shard_map/dot_general | solution.py:43
  97.0 137.0 %all-reduce.4.cloned.1.call-done = f32[1024,512]{0,1:T(8,128)} async-done(((f32[1024,512]{0,1:T(8,128)}), f32[1024,512]{0,1:T(8,128)}) %all-reduce.4.cloned.1.call-update) | async-done | bytes 2097168 | tf_op jit(solution)/shard_map/psum | solution.py:58
  233.9 6.8 %fusion.56 = f32[512,512]{1,0:T(8,128)} fusion(f32[1024,512]{0,1:T(8,128)} %all-reduce.4.cloned.1.call-done), kind=kOutput, calls=%fused_computation.103 | convolution fusion | flops 3221225472 | bytes 3145728 | tf_op jit(solution)/shard_map/dot_general | solution.py:59
  240.7 40.2 %reduce-scatter.2.cloned.1.call-done = bf16[256,512]{1,0:T(8,128)(2,1)} async-done(((bf16[2048,512]{1,0:T(8,128)(2,1)}), bf16[256,512]{1,0:T(8,128)(2,1)}) %reduce-scatter.2.cloned.1.call-update) | async-done | bytes 262160 | tf_op jit(solution)/shard_map/reduce_scatter | solution.py:49
  280.9 3.8 collective-permute-start.1
  284.8 3.4 collective-permute-done.1
  288.2 53.9 %all-gather.6.cloned.1.call-done = f32[4096,512]{1,0:T(8,128)} async-done(((f32[512,512]{1,0:T(8,128)}), f32[4096,512]{1,0:T(8,128)}) %all-gather.6.cloned.1.call-update) | async-done | bytes 8388624 | tf_op jit(solution)/shard_map/all_gather | solution.py:60
  342.1 4.5 reduce_sum.9
  347.2 1.0 copy-done.3
  348.2 11.7 %cholesky.104 = f32[128,128]{1,0:T(8,128)S(1)} custom-call(f32[128,128]{1,0:T(8,128)S(1)} %cholesky.266), custom_call_target="Cholesky" | custom-call | tf_op jit(solution)/shard_map/jit(cholesky)/cholesky | solution.py:22
  360.0 9.8 %custom-call.30 = f32[1,128,128]{1,2,0:T(8,128)S(1)} custom-call(f32[1,128,128]{2,1,0:T(8,128)S(1)} %get-tuple-element.33), custom_call_target="InvertDiagBlocksLowerTriangular" | custom-call | tf_op jit(solution)/shard_map/jit(cholesky)/cholesky | solution.py:22
  369.9 1.2 constant_dynamic-update-slice_fusion.3
  371.1 1.3 convolution_subtract_fusion.2
  372.4 11.9 %cholesky.217 = f32[128,128]{1,0:T(8,128)S(1)} custom-call(f32[128,128]{1,0:T(8,128)S(1)} %cholesky.270), custom_call_target="Cholesky" | custom-call | tf_op jit(solution)/shard_map/jit(cholesky)/cholesky | solution.py:22
  384.3 9.8 %custom-call.31 = f32[1,128,128]{1,2,0:T(8,128)S(1)} custom-call(f32[1,128,128]{2,1,0:T(8,128)S(1)} %get-tuple-element.30), custom_call_target="InvertDiagBlocksLowerTriangular" | custom-call | tf_op jit(solution)/shard_map/jit(cholesky)/cholesky | solution.py:22
  394.4 1.0 copy-done.2
  395.3 1.3 convolution_subtract_fusion.3
  396.7 11.7 %cholesky.238 = f32[128,128]{1,0:T(8,128)S(1)} custom-call(f32[128,128]{1,0:T(8,128)S(1)} %cholesky.275), custom_call_target="Cholesky" | custom-call | tf_op jit(solution)/shard_map/jit(cholesky)/cholesky | solution.py:22
  408.4 0.6 select_reduce_fusion.1
  409.0 0.7 compare_reduce_fusion.1
  409.7 9.8 %custom-call.32 = f32[1,128,128]{1,2,0:T(8,128)S(1)} custom-call(f32[1,128,128]{2,1,0:T(8,128)S(1)} %get-tuple-element.27), custom_call_target="InvertDiagBlocksLowerTriangular" | custom-call | tf_op jit(solution)/shard_map/jit(cholesky)/cholesky | solution.py:22
  419.5 0.8 convolution_dynamic-update-slice_fusion.1
  420.4 1.4 convolution_subtract_fusion.4
  421.8 11.9 %cholesky.255 = f32[128,128]{1,0:T(8,128)S(1)} custom-call(f32[128,128]{1,0:T(8,128)S(1)} %convolution_subtract_fusion.4), custom_call_target="Cholesky" | custom-call | tf_op jit(solution)/shard_map/jit(cholesky)/cholesky | solution.py:22
  433.7 0.7 select_reduce_fusion
  434.4 0.6 compare_reduce_fusion
  435.0 0.7 compare_reduce_fusion.2
  438.2 2.3 select_select_fusion
  440.5 14.1 %while.1 = (s32[]{:T(128)}, f32[512,512]{1,0:T(8,128)}, s32[4,2]{0,1:T(2,128)S(1)}, f32[4,128,128]{2,1,0:T(8,128)}, s32[]{:T(128)}) while((s32[]{:T(128)}, f32[512,512]{1,0:T(8,128)}, s32[4,2]{0,1:T(2,128)S(1)}, f32[4,128,128]{2,1,0:T(8,128)}, s32[]{:T(128)}) %tuple.36), condition=%wide.while_cond, body=%wide.while_body.sunk | while | flops 2 | bytes 132705 | solution.py:23
  441.2 2.9 bitcast_dynamic-update-slice_fusion.2
  444.7 2.9 bitcast_dynamic-update-slice_fusion.2
  448.3 2.9 bitcast_dynamic-update-slice_fusion.2
  451.8 2.8 bitcast_dynamic-update-slice_fusion.2
  454.6 40.1 %custom-call.33 = f32[4,128,128]{1,2,0:T(8,128)S(1)} custom-call(f32[4,128,128]{2,1,0:T(8,128)} %get-tuple-element.9), custom_call_target="InvertDiagBlocksLowerTriangular" | custom-call | tf_op jit(solution)/shard_map/triangular_solve | solution.py:23
  495.4 1.4 convolution_subtract_fusion.1
  497.5 1.6 convolution_subtract_fusion
  499.7 2.0 fusion.7
  502.7 1.3 copy.11
  504.0 0.7 copy.31
  (48 shorter events, 6.8 us)
Async XLA Ops:
  7.2 83.9 %copy-start = (bf16[1,512,1024]{2,1,0:T(8,128)(2,1)S(1)}, bf16[1,512,1024]{2,1,0:T(8,128)(2,1)}, u32[]{:S(2)}) copy-start(bf16[1,512,1024]{2,1,0:T(8,128)(2,1)} %param.10) | copy-start | bytes 3145732
  7.2 8.0 %copy-start.4 = (bf16[1,1024,512]{2,1,0:T(8,128)(2,1)S(1)}, bf16[1,1024,512]{2,1,0:T(8,128)(2,1)}, u32[]{:S(2)}) copy-start(bf16[1,1024,512]{2,1,0:T(8,128)(2,1)} %param.11) | copy-start | bytes 3145732
  7.2 40.0 %copy-start.5 = (bf16[1,128,1024]{2,1,0:T(8,128)(2,1)S(1)}, bf16[1,128,1024]{2,1,0:T(8,128)(2,1)}, u32[]{:S(2)}) copy-start(bf16[1,128,1024]{2,1,0:T(8,128)(2,1)} %param.6) | copy-start | bytes 786436
  7.2 83.8 %all-gather.4.cloned.1.call-start = ((), (), s32[]{:S(2)}) async-start(), calls=%async_computation.1 | async-start | bytes 4456448 | tf_op jit(solution)/shard_map/all_gather | solution.py:44
  8.7 5.5 %collective-permute-start = (f32[3,1024]{1,0:T(4,128)S(1)}, f32[3,1024]{1,0:T(4,128)S(1)}, u32[]{:S(2)}, u32[]{:S(2)}) collective-permute-start(f32[3,1024]{1,0:T(4,128)S(1)} %slice.150), channel_id=1, source_target_pairs={{8,0},{16,8},{24,16},{32,24},{40,32},{48,40},{56,48},{64,56},{72,6... | collective-permute-start | bytes 36872 | tf_op jit(solution)/shard_map/ppermute | solution.py:13
  15.1 218.8 %all-reduce.4.cloned.1.call-start = ((), (), s32[]{:S(2)}) async-start(), calls=%async_computation.3 | async-start | bytes 4194304 | tf_op jit(solution)/shard_map/psum | solution.py:58
  49.0 231.9 %reduce-scatter.2.cloned.1.call-start = ((), (), s32[]{:S(2)}) async-start(), calls=%async_computation.2 | async-start | bytes 2359296 | tf_op jit(solution)/shard_map/reduce_scatter | solution.py:49
  96.9 245.2 %all-gather.6.cloned.1.call-start = ((), (), s32[]{:S(2)}) async-start(), calls=%async_computation.4 | async-start | bytes 9437184 | tf_op jit(solution)/shard_map/all_gather | solution.py:60
  280.9 7.3 %collective-permute-start.1 = (bf16[256,512]{1,0:T(8,128)(2,1)}, bf16[256,512]{1,0:T(8,128)(2,1)S(1)}, u32[]{:S(2)}, u32[]{:S(2)}) collective-permute-start(bf16[256,512]{1,0:T(8,128)(2,1)} %reduce-scatter.2.cloned.1.call-done), channel_id=1, source_target_pairs={{0,384},{128,0},{256,128},{384,256},{1,385},{129,1},{257,129},{385... | collective-permute-start | bytes 786440 | tf_op jit(solution)/shard_map/ppermute | solution.py:18
  288.2 53.9 %copy-start.6 = (bf16[256,512]{1,0:T(8,128)(2,1)}, bf16[256,512]{1,0:T(8,128)(2,1)S(1)}, u32[]{:S(2)}) copy-start(bf16[256,512]{1,0:T(8,128)(2,1)S(1)} %collective-permute-done.1) | copy-start | bytes 786436
  347.2 1.0 copy-start.3
  394.4 1.0 copy-start.2
  396.6 98.1 %copy-start.1 = (f32[1024,512]{0,1:T(8,128)S(1)}, f32[1024,512]{0,1:T(8,128)}, u32[]{:S(2)}) copy-start(f32[1024,512]{0,1:T(8,128)} %all-reduce.4.cloned.1.call-done) | copy-start | bytes 6291460
  502.4 1.6 copy-start.7
Sparse Core Ops, SparseCore 0:
  15.2 75.7 all-gather.3
  93.4 140.5 all-reduce.3
  236.8 44.1 reduce-scatter.1
  283.5 58.5 all-gather.5
